TPU v7x, 32 devices: a whole 2x2x4 slice. The times are simulated.
32 devices in a mesh: region: 2 (over x), space: 16 (over z, y, core).
Axes of the slice: x: 2, y: 2, z: 4, core: 2. Of those that a mesh axis runs over, the one named last changes fastest.
Arguments:
- right_side: float32 [8, 64, 8192], P('region', None, 'space'), parts along dimension 0, may hold values from -45 to 45
- obs_prec: float32 [128, 8192], P('region', 'space'), parts along dimension 0, may hold values from 0.2 to 5
- outlier_flags: int32 [128, 8192], P('region', 'space'), parts along dimension 0, may hold values 0 or 1
- up_one: float32 [64, 256, 128], P('space', 'region'), parts along dimension 1, may hold values from -0.015625 to 0.015625
- up_two: float32 [64, 256, 128], P('space', 'region'), parts along dimension 1, may hold values from -0.015625 to 0.015625
Outputs:
- smoothed: float32 [8, 64, 8192], P('region', None, 'space'), parts along dimension 0
- residual: float32 [8, 64, 8192], P('region', None, 'space'), parts along dimension 0
There are 2 independent parts, one for each index of `region`. A program takes and returns all parts, laid end to end along the dimension named above; each array names one. Nothing has to cross between parts.
All inputs are finite; a program needn't handle non-finite values. No bound on the sum of `outlier_flags` on one device may be relied on, other than what follows from the above.
Results may differ from a plain program's by a relative error of at most 0.0003.
Values sent between devices are 32-bit elements; how exact they have to be, the bound alone decides.
A program may use at most 64 MiB of HBM per device.

v0:
```python
import jax
import jax.numpy as jnp
from jax import lax
from jax.sharding import PartitionSpec as P

TILE = 128
ITERS = 3


def extended(shard, sides, width):
    for axis, dim in sides:
        count, length = (lax.axis_size(axis), shard.shape[dim])
        up = [(i, (i + 1) % count) for i in range(count - 1)]
        down = [(j, i) for i, j in up]
        last = lax.slice_in_dim(shard, length - width, length, axis=dim)
        initial = lax.slice_in_dim(shard, 0, width, axis=dim)
        before = lax.ppermute(last, axis, up)
        after = lax.ppermute(initial, axis, down)
        shard = jnp.concatenate([before, shard, after], axis=dim)
    return shard


def from_behind(value, axis, steps):
    count = lax.axis_size(axis)
    initial, last = (max(0, -steps), min(count, count - steps))
    return lax.ppermute(value, axis, [(source, source + steps) for source in range(initial, last)])


def lagged(field, lag):
    return jnp.concatenate([jnp.zeros_like(field[:, :lag]), field[:, :-lag]], axis=1)


def leading(field, lag):
    return jnp.concatenate([field[:, lag:], jnp.zeros_like(field[:, :lag])], axis=1)


def temporal(field):
    innov = field - 1.5 * lagged(field, 1) + 0.6 * lagged(field, 2)
    return innov - 1.5 * leading(innov, 1) + 0.6 * leading(innov, 2)


def tile_forward(blocks, tiles):
    return jnp.einsum("fdbj,bij->fdbi", blocks, tiles, precision=lax.Precision.HIGHEST)


def tile_backward(blocks, tiles):
    return jnp.einsum("fdbi,bij->fdbj", blocks, tiles, precision=lax.Precision.HIGHEST)


def spatial(field, up_one, up_two, edge_pair):
    nf, nd, ncell = field.shape
    nblk = ncell // TILE
    blocks = field.reshape(nf, nd, nblk, TILE)
    output = 8.0 * blocks
    padded = extended(field, (("space", 2),), 2 * TILE)
    padded = padded.reshape(nf, nd, nblk + 4, TILE)
    for reach, tiles, prior in ((1, up_one, edge_pair[0]), (2, up_two, edge_pair[1])):
        with_prior = jnp.concatenate([prior, tiles], axis=0)
        forward = tile_forward(padded[:, :, 2 + reach : 2 + reach + nblk], tiles)
        backward = tile_backward(
            padded[:, :, 2 - reach : 2 - reach + nblk], with_prior[2 - reach : 2 - reach + nblk]
        )
        output = output - forward - backward
    return output.reshape(nf, nd, ncell)


def field_sums(values):
    return jnp.sum(values, axis=(1, 2))[:, None, None]


def on_device(right_side, obs_prec, outlier_flags, up_one, up_two):
    weight = obs_prec * (1.0 - 0.9 * outlier_flags.astype(jnp.float32))
    edge_pair = from_behind((up_one[-2:], up_two[-2:]), "space", 1)

    def squares(values):
        return lax.psum(field_sums(values * values), "space")

    smoothed = jnp.zeros_like(right_side)
    residual = right_side
    direction = right_side
    norm_now = squares(residual)
    for step in range(ITERS):
        image = (
            weight[None] * direction
            + spatial(direction, up_one, up_two, edge_pair)
            + 0.5 * temporal(direction)
        )
        alpha = norm_now / lax.psum(field_sums(direction * image), "space")
        smoothed = smoothed + alpha * direction
        residual = residual - alpha * image
        norm_next = squares(residual)
        direction = residual + norm_next / norm_now * direction
        norm_now = norm_next
    return (smoothed, residual)


def solution(mesh):
    placed = (
        P("region", None, "space"),
        P("region", "space"),
        P("region", "space"),
        P("space", "region", None),
        P("space", "region", None),
    )
    return jax.shard_map(
        on_device,
        mesh=mesh,
        in_specs=placed,
        out_specs=(P("region", None, "space"), P("region", None, "space")),
        check_vma=False,
    )
```

profile of v0, /device:TPU:0, one launch (start us, length us, event | category | flops | bytes accessed | tf_op | source)
XLA Modules:
  0.0 201.0 jit_solution(11156354566498877640)
XLA Ops:
  0.6 1.1 fusion.35
  1.8 2.5 %collective-permute-start = (f32[4,64,256]{2,1,0:T(8,128)S(1)}, f32[4,64,256]{2,1,0:T(8,128)S(1)}, u32[]{:S(2)}, u32[]{:S(2)}) collective-permute-start(f32[4,64,256]{2,1,0:T(8,128)S(1)} %get-tuple-element.35), channel_id=1, source_target_pairs={{0,1},{1,2},{2,3},{3,4},{4,5},{5,6},{6,7},{7,8},{8,9},{9,10},{10,1... | collective-permute-start | bytes 786440 | tf_op jit(solution)/shard_map/ppermute | solution.py:17
  4.3 1.3 collective-permute-start.1
  5.6 5.2 %collective-permute-start.2 = (f32[2,128,128]{2,1,0:T(8,128)S(1)}, f32[2,128,128]{2,1,0:T(8,128)S(1)}, u32[]{:S(2)}, u32[]{:S(2)}) collective-permute-start(f32[2,128,128]{2,1,0:T(8,128)S(1)} %slice.109), channel_id=1, source_target_pairs={{0,1},{1,2},{2,3},{3,4},{4,5},{5,6},{6,7},{7,8},{8,9},{9,10},{10,1... | collective-permute-start | bytes 393224 | tf_op jit(solution)/shard_map/ppermute | solution.py:26
  10.8 3.6 %collective-permute-start.3 = (f32[2,128,128]{2,1,0:T(8,128)S(1)}, f32[2,128,128]{2,1,0:T(8,128)S(1)}, u32[]{:S(2)}, u32[]{:S(2)}) collective-permute-start(f32[2,128,128]{2,1,0:T(8,128)S(1)} %slice.113), channel_id=1, source_target_pairs={{0,1},{1,2},{2,3},{3,4},{4,5},{5,6},{6,7},{7,8},{8,9},{9,10},{10,1... | collective-permute-start | bytes 393224 | tf_op jit(solution)/shard_map/ppermute | solution.py:26
  14.7 0.7 copy-done.3
  16.6 0.6 fusion.36
  17.2 0.6 fusion
  17.8 0.6 fusion.37
  18.4 0.7 fusion.17
  19.7 32.1 %all-reduce.12 = (f32[4,1,1]{0,2,1:T(1,128)S(1)}, f32[4,1,1]{0,2,1:T(1,128)S(1)}) all-reduce(f32[4,1,1]{0,2,1:T(1,128)S(1)} %bitcast.186, f32[4,1,1]{0,2,1:T(1,128)S(1)} %bitcast.185), channel_id=1, replica_groups=mesh['region'=2,'space'=16] {'space'}, use_global_device_ids=true, to_apply=%region_1.0 | all-reduce | flops 8 | bytes 64 | tf_op jit(solution)/shard_map/psum | solution.py:76
  52.1 29.5 %psum.44 = f32[4,1,1]{0,2,1:T(1,128)S(1)} all-reduce(f32[4,1,1]{0,2,1:T(1,128)S(1)} %bitcast.184), channel_id=1, replica_groups=mesh['region'=2,'space'=16] {'space'}, use_global_device_ids=true, to_apply=%region_5.0 | all-reduce | flops 4 | bytes 32 | tf_op jit(solution)/shard_map/psum | solution.py:76
  81.8 1.8 collective-permute-start.4
  83.6 1.3 collective-permute-start.5
  85.2 1.8 collective-permute-done.5
  87.8 0.6 fusion.39
  88.5 0.6 fusion.38
  89.1 0.6 fusion.1
  89.7 0.7 fusion.12
  90.4 1.1 multiply_reduce_fusion.2
  91.5 33.7 %psum.45 = f32[4,1,1]{0,2,1:T(1,128)S(1)} all-reduce(f32[4,1,1]{0,2,1:T(1,128)S(1)} %bitcast.188), channel_id=1, replica_groups=mesh['region'=2,'space'=16] {'space'}, use_global_device_ids=true, to_apply=%region_7.0 | all-reduce | flops 4 | bytes 32 | tf_op jit(solution)/shard_map/psum | solution.py:88
  125.2 1.3 multiply_reduce_fusion.1
  126.5 29.5 %psum.46 = f32[4,1,1]{0,2,1:T(1,128)S(1)} all-reduce(f32[4,1,1]{0,2,1:T(1,128)S(1)} %bitcast.189), channel_id=1, replica_groups=mesh['region'=2,'space'=16] {'space'}, use_global_device_ids=true, to_apply=%region_9.0 | all-reduce | flops 4 | bytes 32 | tf_op jit(solution)/shard_map/psum | solution.py:76
  156.7 1.8 collective-permute-start.6
  158.5 1.5 collective-permute-start.7
  160.4 1.6 collective-permute-done.7
  162.8 0.6 fusion.41
  163.4 0.6 fusion.40
  164.0 0.6 fusion.2
  164.6 0.7 fusion.7
  165.8 33.9 %psum.47 = f32[4,1,1]{0,2,1:T(1,128)S(1)} all-reduce(f32[4,1,1]{0,2,1:T(1,128)S(1)} %bitcast.187), channel_id=1, replica_groups=mesh['region'=2,'space'=16] {'space'}, use_global_device_ids=true, to_apply=%region_11.0 | all-reduce | flops 4 | bytes 32 | tf_op jit(solution)/shard_map/psum | solution.py:88
  199.7 1.3 multiply_subtract_fusion
  (62 shorter events, 5.8 us)
Async XLA Ops:
  0.6 5.0 %copy-start.1 = (f32[4,128,128]{2,1,0:T(8,128)S(1)}, f32[4,128,128]{2,1,0:T(8,128)}, u32[]{:S(2)}) copy-start(f32[4,128,128]{2,1,0:T(8,128)} %param.8) | copy-start | bytes 786436
  0.6 10.2 %copy-start.2 = (f32[4,128,128]{2,1,0:T(8,128)S(1)}, f32[4,128,128]{2,1,0:T(8,128)}, u32[]{:S(2)}) copy-start(f32[4,128,128]{2,1,0:T(8,128)} %param.9) | copy-start | bytes 786436
  1.8 12.7 %copy-start = (f32[4,64,512]{2,1,0:T(8,128)S(1)}, f32[4,64,512]{2,1,0:T(8,128)}, u32[]{:S(2)}) copy-start(f32[4,64,512]{2,1,0:T(8,128)} %param.5) | copy-start | bytes 1572868
  1.8 13.9 %collective-permute-start = (f32[4,64,256]{2,1,0:T(8,128)S(1)}, f32[4,64,256]{2,1,0:T(8,128)S(1)}, u32[]{:S(2)}, u32[]{:S(2)}) collective-permute-start(f32[4,64,256]{2,1,0:T(8,128)S(1)} %get-tuple-element.35), channel_id=1, source_target_pairs={{0,1},{1,2},{2,3},{3,4},{4,5},{5,6},{6,7},{7,8},{8,9},{9,10},{10,1... | collective-permute-start | bytes 786440 | tf_op jit(solution)/shard_map/ppermute | solution.py:17
  4.3 11.4 %collective-permute-start.1 = (f32[4,64,256]{2,1,0:T(8,128)S(1)}, f32[4,64,256]{2,1,0:T(8,128)S(1)}, u32[]{:S(2)}, u32[]{:S(2)}) collective-permute-start(f32[4,64,256]{2,1,0:T(8,128)S(1)} %get-tuple-element.36), channel_id=1, source_target_pairs={{1,0},{2,1},{3,2},{4,3},{5,4},{6,5},{7,6},{8,7},{9,8},{10,9},{11,1... | collective-permute-start | bytes 786440 | tf_op jit(solution)/shard_map/ppermute | solution.py:18
  5.6 10.0 %collective-permute-start.2 = (f32[2,128,128]{2,1,0:T(8,128)S(1)}, f32[2,128,128]{2,1,0:T(8,128)S(1)}, u32[]{:S(2)}, u32[]{:S(2)}) collective-permute-start(f32[2,128,128]{2,1,0:T(8,128)S(1)} %slice.109), channel_id=1, source_target_pairs={{0,1},{1,2},{2,3},{3,4},{4,5},{5,6},{6,7},{7,8},{8,9},{9,10},{10,1... | collective-permute-start | bytes 393224 | tf_op jit(solution)/shard_map/ppermute | solution.py:26
  10.8 4.8 %collective-permute-start.3 = (f32[2,128,128]{2,1,0:T(8,128)S(1)}, f32[2,128,128]{2,1,0:T(8,128)S(1)}, u32[]{:S(2)}, u32[]{:S(2)}) collective-permute-start(f32[2,128,128]{2,1,0:T(8,128)S(1)} %slice.113), channel_id=1, source_target_pairs={{0,1},{1,2},{2,3},{3,4},{4,5},{5,6},{6,7},{7,8},{8,9},{9,10},{10,1... | collective-permute-start | bytes 393224 | tf_op jit(solution)/shard_map/ppermute | solution.py:26
  14.5 0.9 copy-start.3
  14.5 1.0 copy-start.4
  81.8 3.4 %collective-permute-start.4 = (f32[4,64,256]{2,1,0:T(8,128)S(1)}, f32[4,64,256]{2,1,0:T(8,128)S(1)}, u32[]{:S(2)}, u32[]{:S(2)}) collective-permute-start(f32[4,64,256]{2,1,0:T(8,128)S(1)} %get-tuple-element.31), channel_id=1, source_target_pairs={{0,1},{1,2},{2,3},{3,4},{4,5},{5,6},{6,7},{7,8},{8,9},{9,10},{10,1... | collective-permute-start | bytes 786440 | tf_op jit(solution)/shard_map/ppermute | solution.py:17
  83.6 3.4 %collective-permute-start.5 = (f32[4,64,256]{2,1,0:T(8,128)S(1)}, f32[4,64,256]{2,1,0:T(8,128)S(1)}, u32[]{:S(2)}, u32[]{:S(2)}) collective-permute-start(f32[4,64,256]{2,1,0:T(8,128)S(1)} %get-tuple-element.32), channel_id=1, source_target_pairs={{1,0},{2,1},{3,2},{4,3},{5,4},{6,5},{7,6},{8,7},{9,8},{10,9},{11,1... | collective-permute-start | bytes 786440 | tf_op jit(solution)/shard_map/ppermute | solution.py:18
  156.0 0.5 copy-start.5
  156.7 3.6 %collective-permute-start.6 = (f32[4,64,256]{2,1,0:T(8,128)S(1)}, f32[4,64,256]{2,1,0:T(8,128)S(1)}, u32[]{:S(2)}, u32[]{:S(2)}) collective-permute-start(f32[4,64,256]{2,1,0:T(8,128)S(1)} %get-tuple-element.29), channel_id=1, source_target_pairs={{0,1},{1,2},{2,3},{3,4},{4,5},{5,6},{6,7},{7,8},{8,9},{9,10},{10,1... | collective-permute-start | bytes 786440 | tf_op jit(solution)/shard_map/ppermute | solution.py:17
  158.5 3.4 %collective-permute-start.7 = (f32[4,64,256]{2,1,0:T(8,128)S(1)}, f32[4,64,256]{2,1,0:T(8,128)S(1)}, u32[]{:S(2)}, u32[]{:S(2)}) collective-permute-start(f32[4,64,256]{2,1,0:T(8,128)S(1)} %get-tuple-element.30), channel_id=1, source_target_pairs={{1,0},{2,1},{3,2},{4,3},{5,4},{6,5},{7,6},{8,7},{9,8},{10,9},{11,1... | collective-permute-start | bytes 786440 | tf_op jit(solution)/shard_map/ppermute | solution.py:18
  165.8 33.9 %copy-start.6 = (f32[4,1,1]{0,2,1:T(1,128)S(1)}, f32[4,1,1]{0,2,1:T(1,128)}, u32[]{:S(2)}) copy-start(f32[4,1,1]{0,2,1:T(1,128)} %copy-done.5) | copy-start | bytes 52
where the time goes:
time: 201 us
  blocking collectives  159 us (79%)
  starting transfers between devices  18.9 us (9%)
  matrix products  7.47 us (4%)
  other arithmetic  6.23 us (3%)
  local copies, waits for them, and re-layouts  5.11 us (3%)
  waiting for transfers between devices  3.41 us (2%)
    psum x3, blocking collectives, squares(): return lax.psum(field_sums(values * values), 'space')  91.1 us
    psum x2, blocking collectives, on_device(): alpha = norm_now / lax.psum(field_sums(direction * image), 'space')  67.6 us
    ppermute x2, starting transfers between devices, from_behind(): lax.ppermute(value, axis, [(source, source + steps) for source in range(i...  8.8 us
    ppermute x3, starting transfers between devices, extended(): before = lax.ppermute(last, axis, up)  6.07 us
    ppermute x3, starting transfers between devices, extended(): after = lax.ppermute(initial, axis, down)  4.06 us
  transfers between devices with their start and end apart: 8, of which 2 were waited for; matrix products, arithmetic and copies ran while one was open for 1% of the time, Pallas kernels for 0%

commit v1 on v0

v1 whole, which is shorter than its diff:
```python
import functools

import jax
import jax.numpy as jnp
from jax import lax
from jax.experimental import pallas as pl
from jax.experimental.pallas import tpu as pltpu
from jax.sharding import PartitionSpec as P

TILE = 128
ITERS = 3
GROUPS = 2
PAIR = 2 * TILE
F32 = jnp.float32
BF16 = jnp.bfloat16

FIRST_FIRST, SECOND_FIRST, FIRST_SECOND, SECOND_SECOND, RIGHT_SECOND, SECOND_NEXT = range(6)


def split(x):
    high = x.astype(BF16)
    return high, (x - high.astype(F32)).astype(BF16)


def temporal(x):
    days = x.shape[0]
    row = lax.broadcasted_iota(jnp.int32, x.shape, 0)

    def lagged(v, lag):
        return jnp.where(row >= lag, pltpu.roll(v, lag, 0), 0.0)

    def leading(v, lag):
        return jnp.where(row < days - lag, pltpu.roll(v, days - lag, 0), 0.0)

    innov = x - 1.5 * lagged(x, 1) + 0.6 * lagged(x, 2)
    return innov - 1.5 * leading(innov, 1) + 0.6 * leading(innov, 2)


def kernel(
    n, nf, days,
    rs, prec, flags, one, two,
    x, r,
    high, low, diag, p, w, cs, h_right, h_left, p_right, r_right, p_left, r_left, red,
    send_r, recv_r, send_l, recv_l, send_s, recv_s,
):
    me = lax.axis_index("space")
    per = nf // GROUPS
    rows = per * days
    half = (slice(0, PAIR), slice(PAIR, 2 * PAIR))

    barrier = pltpu.get_barrier_semaphore()

    def greet(step, carry):
        pl.semaphore_signal(
            barrier, inc=1, device_id={"space": lax.rem(me + step, n)},
            device_id_type=pl.DeviceIdType.MESH,
        )
        return carry

    lax.fori_loop(1, n, greet, 0)

    def put(place, a, b, value):
        hi, lo = split(value)
        at = (place, slice(a * TILE, (a + 1) * TILE), slice(b * TILE, (b + 1) * TILE))
        high[at] = hi
        low[at] = lo

    def dot(value, place):
        hi, lo = value
        return (
            jnp.dot(hi, high[place], preferred_element_type=F32)
            + jnp.dot(hi, low[place], preferred_element_type=F32)
            + jnp.dot(lo, high[place], preferred_element_type=F32)
        )

    def of_group(g):
        return slice(g * rows, (g + 1) * rows)

    def of_field(f):
        return slice(f * days, (f + 1) * days)

    def to_prev(e, g):
        src = rs.at[of_group(g), half[0]] if e == 0 else w.at[e - 1, 0, of_group(g)]
        return pltpu.make_async_remote_copy(
            src_ref=src, dst_ref=h_right.at[e, of_group(g)],
            send_sem=send_r.at[e, g], recv_sem=recv_r.at[e, g],
            device_id={"space": jnp.maximum(me - 1, 0)},
            device_id_type=pl.DeviceIdType.MESH,
        )

    def to_next(e, g):
        return pltpu.make_async_remote_copy(
            src_ref=cs.at[e, of_group(g)], dst_ref=h_left.at[e, of_group(g)],
            send_sem=send_l.at[e, g], recv_sem=recv_l.at[e, g],
            device_id={"space": jnp.minimum(me + 1, n - 1)},
            device_id_type=pl.DeviceIdType.MESH,
        )

    zero = jnp.zeros((TILE, TILE), F32)
    put(SECOND_NEXT, 0, 0, two[2])
    put(SECOND_NEXT, 0, 1, zero)
    put(SECOND_NEXT, 1, 0, one[3])
    put(SECOND_NEXT, 1, 1, two[3])
    pl.semaphore_wait(barrier, n - 1)

    for g in range(GROUPS):
        @pl.when(me > 0)
        def _():
            to_prev(0, g).start()

        cs[0, of_group(g)] = dot(split(rs[of_group(g), half[1]]), SECOND_NEXT)

        @pl.when(me < n - 1)
        def _():
            to_next(0, g).start()

    @pl.when(me == 0)
    def _():
        h_left[...] = jnp.zeros_like(h_left)

    @pl.when(me == n - 1)
    def _():
        h_right[...] = jnp.zeros_like(h_right)

    for place, at in ((FIRST_FIRST, 0), (SECOND_SECOND, 2)):
        put(place, 0, 0, zero)
        put(place, 0, 1, one[at])
        put(place, 1, 0, one[at].T)
        put(place, 1, 1, zero)
    put(FIRST_SECOND, 0, 0, two[0])
    put(FIRST_SECOND, 0, 1, zero)
    put(FIRST_SECOND, 1, 0, one[1])
    put(FIRST_SECOND, 1, 1, two[1])
    for place, at in ((SECOND_FIRST, 0), (RIGHT_SECOND, 2)):
        put(place, 0, 0, two[at].T)
        put(place, 0, 1, one[at + 1].T)
        put(place, 1, 0, zero)
        put(place, 1, 1, two[at + 1].T)
    diag[...] = 8.0 + prec[...] * (1.0 - 0.9 * flags[...].astype(F32))

    def sums_wait(j):
        every = red.at[j, pl.ds(0, n - 1)]
        return pltpu.make_async_copy(every, every, recv_s.at[j])

    def sums_sent(j):
        every = red.at[j, pl.ds(0, n - 1)]
        return pltpu.make_async_copy(every, every, send_s.at[j])

    def send_sums(j, parts):
        kinds = len(parts[0])
        flat = [s for field in parts for s in field]
        column = jnp.concatenate([jnp.sum(s, axis=0, keepdims=True) for s in flat], axis=0)
        column = jnp.sum(column, axis=1, keepdims=True)
        shape = (len(flat), TILE)
        keep = lax.broadcasted_iota(jnp.int32, shape, 0) == lax.broadcasted_iota(jnp.int32, shape, 1)
        red[j, me] = jnp.sum(jnp.where(keep, column, 0.0), axis=0, keepdims=True)

        def send(step, carry):
            pltpu.make_async_remote_copy(
                src_ref=red.at[j, me], dst_ref=red.at[j, me],
                send_sem=send_s.at[j], recv_sem=recv_s.at[j],
                device_id={"space": lax.rem(me + step, n)},
                device_id_type=pl.DeviceIdType.MESH,
            ).start()
            return carry

        lax.fori_loop(1, n, send, 0)

    def totals(j, kinds):
        sums_wait(j).wait()
        total = jnp.sum(red[j], axis=0)
        shape = (8, TILE)
        row = lax.broadcasted_iota(jnp.int32, shape, 0)
        lane = lax.broadcasted_iota(jnp.int32, shape, 1)
        total = jnp.broadcast_to(total, shape)
        return [
            jnp.sum(jnp.where(lane == kinds * row + kind, total, 0.0), axis=1, keepdims=True)
            for kind in range(kinds)
        ]

    def fold(a):
        return jnp.sum(a.reshape(days // 8, 8, a.shape[1]), axis=0)

    def folded(a, b):
        s = fold(a * b)
        return s[:, :TILE] + s[:, TILE:]

    for k in range(ITERS):
        last = k == ITERS - 1
        for g in range(GROUPS):
            group = of_group(g)
            j = k * GROUPS + g
            if k == 0:
                p[0, group] = rs[group, half[0]]
                p[1, group] = rs[group, half[1]]
                r[group] = rs[group]
                x[group] = jnp.zeros_like(x[group])
            else:
                rr, pw, rw, ww = totals(j - GROUPS, 4)
                alpha = rr / pw
                beta = (rr + alpha * (alpha * ww - 2.0 * rw)) / rr
                for i in range(per):
                    field = of_field(g * per + i)
                    a, b = alpha[i : i + 1], beta[i : i + 1]
                    for s in range(2):
                        x[field, half[s]] += a * p[s, field]
                        res = r[field, half[s]] - a * w[k - 1, s, field]
                        r[field, half[s]] = res
                        p[s, field] = res + b * p[s, field]
            first, second = split(p[0, group]), split(p[1, group])
            near = dot(first, FIRST_FIRST) + dot(second, SECOND_FIRST)
            far = dot(first, FIRST_SECOND) + dot(second, SECOND_SECOND)
            for i in range(per):
                field = of_field(g * per + i)
                for s, coupled in ((0, near), (1, far)):
                    v = p[s, field]
                    w[k, s, field] = (
                        diag[:, half[s]] * v + 0.5 * temporal(v)
                        - coupled[i * days : (i + 1) * days]
                    )

            @pl.when(me > 0)
            def _():
                to_next(k, g).wait_recv()

            @pl.when(me < n - 1)
            def _():
                to_prev(k, g).wait_recv()

            if k == 0:
                for dst in (p_right, r_right):
                    dst[group] = h_right[k, group]
                for dst in (p_left, r_left):
                    dst[group] = h_left[k, group]
            else:
                for i in range(per):
                    field = of_field(g * per + i)
                    a, b = alpha[i : i + 1], beta[i : i + 1]
                    for pp, res, new in ((p_left, r_left, h_left), (p_right, r_right, h_right)):
                        value = res[field] - a * new[k, field]
                        res[field] = value
                        pp[field] = value + b * pp[field]
            w[k, 0, group] -= p_left[group]
            if not last:
                @pl.when(me > 0)
                def _():
                    to_prev(k + 1, g).start()
            w[k, 1, group] -= dot(split(p_right[group]), RIGHT_SECOND)
            if not last:
                cs[k + 1, group] = dot(split(w[k, 1, group]), SECOND_NEXT)

                @pl.when(me < n - 1)
                def _():
                    to_next(k + 1, g).start()

            parts = []
            for i in range(per):
                field = of_field(g * per + i)
                sums = [0.0] * (2 if last else 4)
                for s in range(2):
                    image, res = w[k, s, field], r[field, half[s]]
                    sums[0] += folded(res, res)
                    sums[1] += folded(p[s, field], image)
                    if not last:
                        sums[2] += folded(res, image)
                        sums[3] += folded(image, image)
                parts.append(sums)
            send_sums(j, parts)

    for g in range(GROUPS):
        rr, pw = totals((ITERS - 1) * GROUPS + g, 2)
        alpha = rr / pw
        for i in range(per):
            field = of_field(g * per + i)
            a = alpha[i : i + 1]
            for s in range(2):
                x[field, half[s]] += a * p[s, field]
                r[field, half[s]] -= a * w[ITERS - 1, s, field]

    for k in range(ITERS):
        for g in range(GROUPS):
            @pl.when(me > 0)
            def _():
                to_prev(k, g).wait_send()

            @pl.when(me < n - 1)
            def _():
                to_next(k, g).wait_send()

            sums_sent(k * GROUPS + g).wait()


def on_device(n, right_side, obs_prec, outlier_flags, up_one, up_two):
    nf, days, cells = right_side.shape
    rows = nf * days
    vmem = pl.BlockSpec(memory_space=pltpu.VMEM)
    side = pltpu.VMEM((rows, PAIR), F32)
    sides = pltpu.VMEM((ITERS, rows, PAIR), F32)
    dma = pltpu.SemaphoreType.DMA
    smoothed, residual = pl.pallas_call(
        functools.partial(kernel, n, nf, days),
        out_shape=[jax.ShapeDtypeStruct((rows, cells), F32)] * 2,
        in_specs=[vmem] * 5,
        out_specs=[vmem] * 2,
        scratch_shapes=[
            pltpu.VMEM((6, PAIR, PAIR), BF16),
            pltpu.VMEM((6, PAIR, PAIR), BF16),
            pltpu.VMEM((days, cells), F32),
            pltpu.VMEM((2, rows, PAIR), F32),
            pltpu.VMEM((ITERS, 2, rows, PAIR), F32),
            sides, sides, sides,
            side, side, side, side,
            pltpu.VMEM((ITERS * GROUPS, n, 1, TILE), F32),
            dma((ITERS, GROUPS)), dma((ITERS, GROUPS)),
            dma((ITERS, GROUPS)), dma((ITERS, GROUPS)),
            dma((ITERS * GROUPS,)), dma((ITERS * GROUPS,)),
        ],
        compiler_params=pltpu.CompilerParams(
            collective_id=0, has_side_effects=True, vmem_limit_bytes=40 * 2**20
        ),
        cost_estimate=pl.CostEstimate(
            flops=36 * ITERS * rows * PAIR * PAIR, bytes_accessed=12 * rows * cells, transcendentals=0
        ),
    )(right_side.reshape(rows, cells), obs_prec, outlier_flags, up_one, up_two)
    shape = (nf, days, cells)
    return smoothed.reshape(shape), residual.reshape(shape)


def solution(mesh):
    placed = (
        P("region", None, "space"),
        P("region", "space"),
        P("region", "space"),
        P("space", "region", None),
        P("space", "region", None),
    )
    return jax.shard_map(
        functools.partial(on_device, mesh.shape["space"]),
        mesh=mesh,
        in_specs=placed,
        out_specs=(P("region", None, "space"), P("region", None, "space")),
        check_vma=False,
    )
```

time: 201 us -> 38.5 us (0.19)
  blocking collectives: 159 us -> 0 us
  Pallas kernels: 0 us -> 31.3 us
  starting transfers between devices: 18.9 us -> 0 us
  matrix products: 7.47 us -> 0 us
  other arithmetic: 6.23 us -> 0 us
  waiting for transfers between devices: 3.41 us -> 0 us
    psum x5 -> x0, blocking collectives: 159 us -> none  [the longest x3 91.1 us: squares(): return lax.psum(field_sums(values * values), 'space')]
    pallas_call x0 -> x1, Pallas kernels: none -> 31.3 us  [on_device(): pl.pallas_call(functools.partial(kernel, n, nf, days), out_shape=[jax.Sha...]
    ppermute x8 -> x0, starting transfers between devices: 18.9 us -> none  [the longest x2 8.8 us: from_behind(): lax.ppermute(value, axis, [(source, source + steps) for source in range(i...]
    unnamed x25 -> x12, local copies, waits for them, and re-layouts: 2.18 us -> 6.33 us
    dot_general x6 -> x0, matrix products: 3.9 us -> none  [tile_forward(): jnp.einsum('fdbj,bij->fdbi', blocks, tiles, precision=lax.Precision.HIGHEST)]
    reduce_sum x5 -> x0, other arithmetic: 3.65 us -> none  [field_sums(): return jnp.sum(values, axis=(1, 2))[:, None, None]]
    unnamed x6 -> x0, matrix products: 3.57 us -> none
    ppermute x8 -> x0, waiting for transfers between devices: 3.41 us -> none  [the longest x3 3.4 us: extended(): after = lax.ppermute(initial, axis, down)]
  transfers between devices with their start and end apart: 8 -> 0, of which waited for: 2 -> 0; matrix products, arithmetic and copies ran while one was open for 1% -> 0% of each run, Pallas kernels for 0% -> 0%
where the time goes in v1:
time: 38.5 us; the launch traced here: 38.3 us
  Pallas kernels  31.3 us (81%)
  local copies, waits for them, and re-layouts  6.33 us (16%)
  between operations  0.65 us (2%)
    pallas_call x1, Pallas kernels, on_device(): pl.pallas_call(functools.partial(kernel, n, nf, days), out_shape=[jax.Sha...  31.3 us
    unnamed x12, local copies, waits for them, and re-layouts  6.33 us

profile of v1, /device:TPU:0, one launch (start us, length us, event | category | flops | bytes accessed | tf_op | source)
XLA Modules:
  0.0 38.3 jit_solution(13659762067927567538)
XLA Ops:
  0.6 0.0 copy-start
  0.6 1.0 %copy-done = f32[4,64,512]{2,1,0:T(8,128)S(1)} copy-done((f32[4,64,512]{2,1,0:T(8,128)S(1)}, f32[4,64,512]{2,1,0:T(8,128)}, u32[]{:S(2)}) %copy-start) | copy-done | bytes 524312
  1.7 0.0 copy-start.1
  1.7 0.9 %copy-done.1 = f32[4,128,128]{2,1,0:T(8,128)S(1)} copy-done((f32[4,128,128]{2,1,0:T(8,128)S(1)}, f32[4,128,128]{2,1,0:T(8,128)}, u32[]{:S(2)}) %copy-start.1) | copy-done | bytes 262168
  2.6 0.0 copy-start.2
  2.6 0.9 %copy-done.2 = f32[4,128,128]{2,1,0:T(8,128)S(1)} copy-done((f32[4,128,128]{2,1,0:T(8,128)S(1)}, f32[4,128,128]{2,1,0:T(8,128)}, u32[]{:S(2)}) %copy-start.2) | copy-done | bytes 262168
  3.6 0.0 copy-start.3
  3.6 0.9 %copy-done.3 = f32[64,512]{1,0:T(8,128)S(1)} copy-done((f32[64,512]{1,0:T(8,128)S(1)}, f32[64,512]{1,0:T(8,128)}, u32[]{:S(2)}) %copy-start.3) | copy-done | bytes 131096
  4.5 0.0 copy-start.4
  4.5 0.9 %copy-done.4 = s32[64,512]{1,0:T(8,128)S(1)} copy-done((s32[64,512]{1,0:T(8,128)S(1)}, s32[64,512]{1,0:T(8,128)}, u32[]{:S(2)}) %copy-start.4) | copy-done | bytes 131096
  5.4 31.3 %shard_map.68 = (f32[256,512]{1,0:T(8,128)S(1)}, f32[256,512]{1,0:T(8,128)S(1)}) custom-call(f32[256,512]{1,0:T(8,128)S(1)} %bitcast.5, f32[64,512]{1,0:T(8,128)S(1)} %copy-done.3, s32[64,512]{1,0:T(8,128)S(1)} %copy-done.4, f32[4,128,128]{2,1,0:T(8,128)S(1)} %copy-done.1, f32[4,128,128]{2,1,0:T(8,128)S(1)} %copy-done.2), custom_call_target="tpu_custom_call" | custom-call | flops 1811939328 | bytes 1572864 | tf_op jit(solution)/shard_map/pallas_call | solution.py:300
  36.7 0.8 %copy.9 = f32[4,64,512]{2,1,0:T(8,128)} copy(f32[4,64,512]{2,1,0:T(8,128)S(1)} %bitcast.4) | data formatting | bytes 1048576
  37.5 0.8 %copy.10 = f32[4,64,512]{2,1,0:T(8,128)} copy(f32[4,64,512]{2,1,0:T(8,128)S(1)} %bitcast.3) | data formatting | bytes 1048576
Async XLA Ops:
  0.6 1.0 %copy-start = (f32[4,64,512]{2,1,0:T(8,128)S(1)}, f32[4,64,512]{2,1,0:T(8,128)}, u32[]{:S(2)}) copy-start(f32[4,64,512]{2,1,0:T(8,128)} %param.5) | copy-start | bytes 1572868
  1.7 0.9 %copy-start.1 = (f32[4,128,128]{2,1,0:T(8,128)S(1)}, f32[4,128,128]{2,1,0:T(8,128)}, u32[]{:S(2)}) copy-start(f32[4,128,128]{2,1,0:T(8,128)} %one.1) | copy-start | bytes 786436
  2.6 0.9 %copy-start.2 = (f32[4,128,128]{2,1,0:T(8,128)S(1)}, f32[4,128,128]{2,1,0:T(8,128)}, u32[]{:S(2)}) copy-start(f32[4,128,128]{2,1,0:T(8,128)} %two.1) | copy-start | bytes 786436
  3.6 0.9 %copy-start.3 = (f32[64,512]{1,0:T(8,128)S(1)}, f32[64,512]{1,0:T(8,128)}, u32[]{:S(2)}) copy-start(f32[64,512]{1,0:T(8,128)} %prec.1) | copy-start | bytes 393220
  4.5 0.9 %copy-start.4 = (s32[64,512]{1,0:T(8,128)S(1)}, s32[64,512]{1,0:T(8,128)}, u32[]{:S(2)}) copy-start(s32[64,512]{1,0:T(8,128)} %flags.1) | copy-start | bytes 393220

commit v2 on v1

--- a/solution.py
+++ b/solution.py
@@ -9,7 +9,7 @@
 
 TILE = 128
 ITERS = 3
-GROUPS = 2
+GROUPS = 4
 PAIR = 2 * TILE
 F32 = jnp.float32
 BF16 = jnp.bfloat16
@@ -38,15 +38,25 @@
 
 def kernel(
     n, nf, days,
+    rs_hbm, prec_hbm, flags_hbm, one_hbm, two_hbm,
+    x, r,
     rs, prec, flags, one, two,
-    x, r,
     high, low, diag, p, w, cs, h_right, h_left, p_right, r_right, p_left, r_left, red,
-    send_r, recv_r, send_l, recv_l, send_s, recv_s,
+    send_r, recv_r, send_l, recv_l, send_s, recv_s, load,
 ):
     me = lax.axis_index("space")
     per = nf // GROUPS
     rows = per * days
     half = (slice(0, PAIR), slice(PAIR, 2 * PAIR))
+
+    loads = [
+        pltpu.make_async_copy(src, dst, load.at[i])
+        for i, (src, dst) in enumerate(
+            ((two_hbm, two), (one_hbm, one), (rs_hbm, rs), (prec_hbm, prec), (flags_hbm, flags))
+        )
+    ]
+    for copy in loads:
+        copy.start()
 
     barrier = pltpu.get_barrier_semaphore()
 
@@ -97,6 +107,8 @@
         )
 
     zero = jnp.zeros((TILE, TILE), F32)
+    for copy in loads:
+        copy.wait()
     put(SECOND_NEXT, 0, 0, two[2])
     put(SECOND_NEXT, 0, 1, zero)
     put(SECOND_NEXT, 1, 0, one[3])
@@ -147,7 +159,6 @@
         return pltpu.make_async_copy(every, every, send_s.at[j])
 
     def send_sums(j, parts):
-        kinds = len(parts[0])
         flat = [s for field in parts for s in field]
         column = jnp.concatenate([jnp.sum(s, axis=0, keepdims=True) for s in flat], axis=0)
         column = jnp.sum(column, axis=1, keepdims=True)
@@ -185,17 +196,18 @@
         s = fold(a * b)
         return s[:, :TILE] + s[:, TILE:]
 
+    def direction(k, s, at):
+        return rs[at, half[s]] if k == 0 else p[s, at]
+
+    def residue(k, s, at):
+        return (rs if k == 0 else r)[at, half[s]]
+
     for k in range(ITERS):
         last = k == ITERS - 1
         for g in range(GROUPS):
             group = of_group(g)
             j = k * GROUPS + g
-            if k == 0:
-                p[0, group] = rs[group, half[0]]
-                p[1, group] = rs[group, half[1]]
-                r[group] = rs[group]
-                x[group] = jnp.zeros_like(x[group])
-            else:
+            if k > 0:
                 rr, pw, rw, ww = totals(j - GROUPS, 4)
                 alpha = rr / pw
                 beta = (rr + alpha * (alpha * ww - 2.0 * rw)) / rr
@@ -203,17 +215,21 @@
                     field = of_field(g * per + i)
                     a, b = alpha[i : i + 1], beta[i : i + 1]
                     for s in range(2):
-                        x[field, half[s]] += a * p[s, field]
-                        res = r[field, half[s]] - a * w[k - 1, s, field]
+                        old = direction(k - 1, s, field)
+                        if k == 1:
+                            x[field, half[s]] = a * old
+                        else:
+                            x[field, half[s]] += a * old
+                        res = residue(k - 1, s, field) - a * w[k - 1, s, field]
                         r[field, half[s]] = res
-                        p[s, field] = res + b * p[s, field]
-            first, second = split(p[0, group]), split(p[1, group])
+                        p[s, field] = res + b * old
+            first, second = (split(direction(k, s, group)) for s in range(2))
             near = dot(first, FIRST_FIRST) + dot(second, SECOND_FIRST)
             far = dot(first, FIRST_SECOND) + dot(second, SECOND_SECOND)
             for i in range(per):
                 field = of_field(g * per + i)
                 for s, coupled in ((0, near), (1, far)):
-                    v = p[s, field]
+                    v = direction(k, s, field)
                     w[k, s, field] = (
                         diag[:, half[s]] * v + 0.5 * temporal(v)
                         - coupled[i * days : (i + 1) * days]
@@ -241,31 +257,31 @@
                         res[field] = value
                         pp[field] = value + b * pp[field]
             w[k, 0, group] -= p_left[group]
-            if not last:
-                @pl.when(me > 0)
-                def _():
-                    to_prev(k + 1, g).start()
             w[k, 1, group] -= dot(split(p_right[group]), RIGHT_SECOND)
             if not last:
                 cs[k + 1, group] = dot(split(w[k, 1, group]), SECOND_NEXT)
-
-                @pl.when(me < n - 1)
-                def _():
-                    to_next(k + 1, g).start()
 
             parts = []
             for i in range(per):
                 field = of_field(g * per + i)
                 sums = [0.0] * (2 if last else 4)
                 for s in range(2):
-                    image, res = w[k, s, field], r[field, half[s]]
+                    image, res = w[k, s, field], residue(k, s, field)
                     sums[0] += folded(res, res)
-                    sums[1] += folded(p[s, field], image)
+                    sums[1] += folded(direction(k, s, field), image)
                     if not last:
                         sums[2] += folded(res, image)
                         sums[3] += folded(image, image)
                 parts.append(sums)
             send_sums(j, parts)
+            if not last:
+                @pl.when(me > 0)
+                def _():
+                    to_prev(k + 1, g).start()
+
+                @pl.when(me < n - 1)
+                def _():
+                    to_next(k + 1, g).start()
 
     for g in range(GROUPS):
         rr, pw = totals((ITERS - 1) * GROUPS + g, 2)
@@ -300,9 +316,14 @@
     smoothed, residual = pl.pallas_call(
         functools.partial(kernel, n, nf, days),
         out_shape=[jax.ShapeDtypeStruct((rows, cells), F32)] * 2,
-        in_specs=[vmem] * 5,
+        in_specs=[pl.BlockSpec(memory_space=pltpu.HBM)] * 5,
         out_specs=[vmem] * 2,
         scratch_shapes=[
+            pltpu.VMEM((rows, cells), F32),
+            pltpu.VMEM(obs_prec.shape, F32),
+            pltpu.VMEM(outlier_flags.shape, jnp.int32),
+            pltpu.VMEM(up_one.shape, F32),
+            pltpu.VMEM(up_two.shape, F32),
             pltpu.VMEM((6, PAIR, PAIR), BF16),
             pltpu.VMEM((6, PAIR, PAIR), BF16),
             pltpu.VMEM((days, cells), F32),
@@ -313,10 +334,10 @@
             pltpu.VMEM((ITERS * GROUPS, n, 1, TILE), F32),
             dma((ITERS, GROUPS)), dma((ITERS, GROUPS)),
             dma((ITERS, GROUPS)), dma((ITERS, GROUPS)),
-            dma((ITERS * GROUPS,)), dma((ITERS * GROUPS,)),
+            dma((ITERS * GROUPS,)), dma((ITERS * GROUPS,)), dma((5,)),
         ],
         compiler_params=pltpu.CompilerParams(
-            collective_id=0, has_side_effects=True, vmem_limit_bytes=40 * 2**20
+            collective_id=0, has_side_effects=True, vmem_limit_bytes=63 * 2**20
         ),
         cost_estimate=pl.CostEstimate(
             flops=36 * ITERS * rows * PAIR * PAIR, bytes_accessed=12 * rows * cells, transcendentals=0

time: 38.5 us -> 35.5 us (0.922)
  local copies, waits for them, and re-layouts: 6.33 us -> 2.72 us
  Pallas kernels: 31.3 us -> 31.9 us
    unnamed x12 -> x4, local copies, waits for them, and re-layouts: 6.33 us -> 2.72 us
    pallas_call x1, Pallas kernels: 31.3 us -> 31.9 us  [on_device(): pl.pallas_call(functools.partial(kernel, n, nf, days), out_shape=[jax.Sha...]
where the time goes in v2:
time: 35.5 us; the launch traced here: 35.3 us
  Pallas kernels  31.9 us (90%)
  local copies, waits for them, and re-layouts  2.72 us (8%)
  between operations  0.65 us (2%)
    pallas_call x1, Pallas kernels, on_device(): pl.pallas_call(functools.partial(kernel, n, nf, days), out_shape=[jax.Sha...  31.9 us
    unnamed x4, local copies, waits for them, and re-layouts  2.72 us

profile of v2, /device:TPU:0, one launch (start us, length us, event | category | flops | bytes accessed | tf_op | source)
XLA Modules:
  0.0 35.3 jit_solution(4940494547832782293)
XLA Ops:
  0.6 31.9 %shard_map.68 = (f32[256,512]{1,0:T(8,128)}, f32[256,512]{1,0:T(8,128)}) custom-call(f32[256,512]{1,0:T(8,128)} %bitcast.5, f32[64,512]{1,0:T(8,128)} %prec_hbm.1, s32[64,512]{1,0:T(8,128)} %flags_hbm.1, f32[4,128,128]{2,1,0:T(8,128)} %one_hbm.1, f32[4,128,128]{2,1,0:T(8,128)} %two_hbm.1), custom_call_target="tpu_custom_call" | custom-call | flops 1811939328 | bytes 1572864 | tf_op jit(solution)/shard_map/pallas_call | solution.py:316
  32.6 0.0 copy-start
  32.6 1.9 %copy.9 = f32[4,64,512]{2,1,0:T(8,128)} copy(f32[4,64,512]{2,1,0:T(8,128)} %bitcast.4) | data formatting | bytes 1048576
  34.5 0.0 copy-done
  34.5 0.8 %copy.10 = f32[4,64,512]{2,1,0:T(8,128)} copy(f32[4,64,512]{2,1,0:T(8,128)S(1)} %bitcast.3) | data formatting | bytes 1048576
Async XLA Ops:
  32.6 1.9 %copy-start = (f32[256,512]{1,0:T(8,128)S(1)}, f32[256,512]{1,0:T(8,128)}, u32[]{:S(2)}) copy-start(f32[256,512]{1,0:T(8,128)} %get-tuple-element.5) | copy-start | bytes 1572868

commit v3 on v2

--- a/solution.py
+++ b/solution.py
@@ -90,7 +90,7 @@
         return slice(f * days, (f + 1) * days)
 
     def to_prev(e, g):
-        src = rs.at[of_group(g), half[0]] if e == 0 else w.at[e - 1, 0, of_group(g)]
+        src = rs_hbm.at[of_group(g), half[0]] if e == 0 else w.at[e - 1, 0, of_group(g)]
         return pltpu.make_async_remote_copy(
             src_ref=src, dst_ref=h_right.at[e, of_group(g)],
             send_sem=send_r.at[e, g], recv_sem=recv_r.at[e, g],

time: 35.5 us -> 35.5 us (level)
  no operation moved by 1% of the time
where the time goes in v3:
time: 35.5 us; the launch traced here: 35.3 us
  Pallas kernels  31.9 us (90%)
  local copies, waits for them, and re-layouts  2.72 us (8%)
  between operations  0.65 us (2%)
    pallas_call x1, Pallas kernels, on_device(): pl.pallas_call(functools.partial(kernel, n, nf, days), out_shape=[jax.Sha...  31.9 us
    unnamed x4, local copies, waits for them, and re-layouts  2.72 us

profile of v3, /device:TPU:0, one launch (start us, length us, event | category | flops | bytes accessed | tf_op | source)
XLA Modules:
  0.0 35.3 jit_solution(10569388963309852010)
XLA Ops:
  0.6 31.9 %shard_map.68 = (f32[256,512]{1,0:T(8,128)}, f32[256,512]{1,0:T(8,128)}) custom-call(f32[256,512]{1,0:T(8,128)} %bitcast.5, f32[64,512]{1,0:T(8,128)} %prec_hbm.1, s32[64,512]{1,0:T(8,128)} %flags_hbm.1, f32[4,128,128]{2,1,0:T(8,128)} %one_hbm.1, f32[4,128,128]{2,1,0:T(8,128)} %two_hbm.1), custom_call_target="tpu_custom_call" | custom-call | flops 1811939328 | bytes 1572864 | tf_op jit(solution)/shard_map/pallas_call | solution.py:316
  32.6 0.0 copy-start
  32.6 1.9 %copy.9 = f32[4,64,512]{2,1,0:T(8,128)} copy(f32[4,64,512]{2,1,0:T(8,128)} %bitcast.4) | data formatting | bytes 1048576
  34.5 0.0 copy-done
  34.5 0.8 %copy.10 = f32[4,64,512]{2,1,0:T(8,128)} copy(f32[4,64,512]{2,1,0:T(8,128)S(1)} %bitcast.3) | data formatting | bytes 1048576
Async XLA Ops:
  32.6 1.9 %copy-start = (f32[256,512]{1,0:T(8,128)S(1)}, f32[256,512]{1,0:T(8,128)}, u32[]{:S(2)}) copy-start(f32[256,512]{1,0:T(8,128)} %get-tuple-element.5) | copy-start | bytes 1572868
